TPU v7x, 256 devices: a whole 4x4x8 slice. The times are simulated.
256 devices in a mesh: chan: 32 (over z_lo, x, core), stn: 8 (over z_hi, y).
Axes of the slice: x: 4, y: 4, z: 8 (z_hi: 2, z_lo: 4; z = z_hi * 4 + z_lo), core: 2. Of those that a mesh axis runs over, the one named last changes fastest.
Arguments:
- samples: bfloat16 [2, 1024, 393216], P(None, 'stn', 'chan'), may hold values from -6 to 6
- chan_index: int32 [512], replicated, may hold values from 0 to 4095, as said below
- flags: int32 [512, 512], P('stn'), may hold values 0 or 1
Outputs:
- visibility: bfloat16 [512, 2, 1024, 640], P('chan', None, 'stn')
Inputs may be any that keep to these rules, and one draw needn't show every extreme that they name: `chan_index`: 512 distinct channel numbers; 0 and 4095 are among them.
All inputs are finite; a program needn't handle non-finite values. No bound on the sum of `flags` on one device may be relied on, other than what follows from the above.
Results may differ from a plain program's by a relative error of at most 0.0073.
Values may be sent and summed in bfloat16 or wider, within the bound.
A program may use at most 64 MiB of HBM per device.

v0:
```python
import math

import jax
import jax.numpy as jnp
from jax import lax
from jax.sharding import PartitionSpec as P

DFT_LEN = 4096
TAPS = 4


def from_behind(block, axis, distance):
    devices = range(lax.axis_size(axis))
    route = [(i - distance, i) for i in devices if i - distance in devices]
    return lax.ppermute(block, axis, route)


def window_table(tap_count, dft_length):
    sample_pos = jnp.arange(tap_count * dft_length, dtype=jnp.float32) + 0.5
    weights = jnp.sinc(sample_pos / dft_length - tap_count / 2.0)
    weights = weights * (0.5 - 0.5 * jnp.cos(2.0 * math.pi / (tap_count * dft_length) * sample_pos))
    weights = weights / jnp.sqrt(jnp.sum(weights * weights))
    return weights.reshape(tap_count, dft_length)


def dft_tables(chan_index, dft_length):
    row_index = jnp.arange(dft_length, dtype=jnp.int32)[:, None]
    phase_index = row_index * chan_index[None, :] % dft_length
    angles = phase_index.astype(jnp.float32) * (2.0 * math.pi / dft_length)
    return (jnp.cos(angles).astype(jnp.bfloat16), jnp.sin(angles).astype(jnp.bfloat16))


def transform(frames, cosine, sine_table):
    contract = (((0,), (3,)), ((), ()))
    along_cos = lax.dot_general(cosine, frames, contract, preferred_element_type=jnp.float32)
    along_sin = lax.dot_general(sine_table, frames, contract, preferred_element_type=jnp.float32)
    return jnp.stack(
        [along_cos[:, :, 0] + along_sin[:, :, 1], along_cos[:, :, 1] - along_sin[:, :, 0]], axis=2
    )


def carry_frames(tail_frames, window, lead_count):
    zero_frames = jnp.zeros_like(tail_frames)
    stretched = jnp.concatenate([tail_frames, zero_frames], axis=2)
    carried = jnp.zeros(tail_frames.shape, jnp.float32)
    for tap_index in range(lead_count):
        carried = (
            carried
            + stretched[:, :, tap_index : tap_index + lead_count, :].astype(jnp.float32)
            * window[tap_index]
        )
    return jnp.transpose(carried, (2, 0, 1, 3)).astype(jnp.bfloat16)


def on_device(samples, chan_index, flags):
    block_size = samples.shape[1]
    total_time = samples.shape[2]
    dft_length = DFT_LEN
    tap_count = TAPS
    lead_count = tap_count - 1
    spec_count = total_time // dft_length
    window = window_table(tap_count, dft_length)
    cosine, sine_table = dft_tables(chan_index, dft_length)
    own_frames = samples.reshape(2, block_size, spec_count, dft_length)
    local_pad = jnp.concatenate(
        [jnp.zeros((2, block_size, lead_count, dft_length), samples.dtype), own_frames], axis=2
    )
    current = jnp.zeros((2, block_size, spec_count, dft_length), jnp.float32)
    for tap_index in range(tap_count):
        current = (
            current
            + local_pad[:, :, tap_index : tap_index + spec_count, :].astype(jnp.float32)
            * window[tap_index]
        )
    current = jnp.transpose(current, (2, 0, 1, 3)).astype(jnp.bfloat16)
    main_part = transform(current, cosine, sine_table)
    received = from_behind(own_frames, "chan", 1)
    extra_part = transform(carry_frames(received, window, lead_count), cosine, sine_table)
    spectra = jnp.concatenate([main_part + extra_part, main_part[:, lead_count:]], axis=1)
    spectra = spectra.astype(jnp.bfloat16)
    turned = lax.all_to_all(spectra, "chan", split_axis=0, concat_axis=1, tiled=True)
    num_blocks = lax.axis_size("stn")
    own_index = lax.axis_index("stn")
    col_count = num_blocks // 2 + 1
    everyone = lax.all_gather(turned, "stn", axis=3, tiled=True)
    pieces = [
        lax.dynamic_slice_in_dim(
            everyone, (own_index - offset + num_blocks) % num_blocks * block_size, block_size, 3
        )
        for offset in range(col_count)
    ]
    columns = jnp.concatenate(pieces, axis=3)
    swapped = jnp.stack([turned[:, :, 1], -turned[:, :, 0]], axis=2)
    real_part = jnp.einsum("ctra,ctrb->cab", turned, columns, preferred_element_type=jnp.float32)
    imag_part = jnp.einsum("ctra,ctrb->cab", swapped, columns, preferred_element_type=jnp.float32)
    half_block = block_size // 2
    strips = [
        lax.dynamic_slice_in_dim(
            flags, (own_index - offset + num_blocks) % num_blocks * half_block, half_block, 1
        )
        for offset in range(col_count)
    ]
    keep_mask = (1 - jnp.concatenate(strips, axis=1)).astype(jnp.float32)
    keep_mask = jnp.repeat(jnp.repeat(keep_mask, 2, axis=0), 2, axis=1)
    total_spectra = turned.shape[1]
    visibility = jnp.stack([real_part, imag_part], axis=1) * keep_mask / total_spectra
    return visibility.astype(jnp.bfloat16)


def solution(mesh):
    in_specs = (P(None, "stn", "chan"), P(), P("stn", None))
    out_specs = P("chan", None, "stn", None)
    return jax.shard_map(
        on_device, mesh=mesh, in_specs=in_specs, out_specs=out_specs, check_vma=False
    )
```

profile of v0, /device:TPU:1, one launch (start us, length us, event | category | flops | bytes accessed | tf_op | source)
XLA Modules:
  0.0 375.2 jit_solution(14467493434903345234)
XLA Ops:
  6.5 8.6 %copy.35 = bf16[2,128,12288]{1,2,0:T(8,128)(2,1)} copy(bf16[2,128,12288]{2,1,0:T(8,128)(2,1)} %param.3) | data formatting | bytes 12582912 | tf_op args[0]
  15.2 4.5 %collective-permute-start = (bf16[2,128,3,4096]{1,3,2,0:T(8,128)(2,1)}, bf16[2,128,3,4096]{1,3,2,0:T(8,128)(2,1)}, u32[]{:S(2)}, u32[]{:S(2)}) collective-permute-start(bf16[2,128,3,4096]{1,3,2,0:T(8,128)(2,1)} %bitcast.44), channel_id=1, source_target_pairs={{0,8},{8,16},{16,24},{24,32},{32,40},{40,48},{48,56},{56,64},{64,7... | collective-permute-start | bytes 18874376 | tf_op jit(solution)/shard_map/ppermute | solution.py:15
  19.7 0.9 multiply_reduce_fusion
  21.3 0.3 broadcast_divide_fusion
  21.7 32.0 %fusion.69 = bf16[4096,512,1,1]{0,1,3,2:T(8,128)(2,1)S(1)} fusion(s32[512]{0:T(512)S(1)} %copy-done.1), kind=kLoop, calls=%fused_computation.31.clone.clone.1 | loop fusion | flops 31457280 | bytes 4196352 | tf_op jit(solution)/shard_map/dot_general | solution.py:36
  53.7 31.7 %fusion.71 = bf16[4096,512,1,1]{0,1,3,2:T(8,128)(2,1)S(1)} fusion(s32[512]{0:T(512)S(1)} %copy-done.1), kind=kLoop, calls=%fused_computation.30.clone.clone.1 | loop fusion | flops 31457280 | bytes 4196352 | tf_op jit(solution)/shard_map/dot_general | solution.py:35
  85.4 32.0 %fusion.73 = bf16[4096,512,1,1]{0,1,3,2:T(8,128)(2,1)S(1)} fusion(s32[512]{0:T(512)S(1)} %copy-done.1), kind=kLoop, calls=%fused_computation.31.clone.1.clone | loop fusion | flops 31457280 | bytes 4196352 | tf_op jit(solution)/shard_map/dot_general | solution.py:36
  117.4 31.7 %fusion.75 = bf16[4096,512,1,1]{0,1,3,2:T(8,128)(2,1)S(1)} fusion(s32[512]{0:T(512)S(1)} %copy-done.1), kind=kLoop, calls=%fused_computation.30.clone.1.clone | loop fusion | flops 31457280 | bytes 4196352 | tf_op jit(solution)/shard_map/dot_general | solution.py:35
  149.2 9.2 %fusion.9 = (bf16[3,2,128,4096]{2,3,0,1:T(8,128)(2,1)S(1)}, bf16[3,2,128,4096]{2,3,0,1:T(8,128)(2,1)S(1)}) fusion(bf16[2,128,3,4096]{1,3,2,0:T(8,128)(2,1)} %collective-permute-done, f32[4096]{0:T(1024)S(1)} %get-tuple-element.16, f32[4096]{0:T(1024)S(1)} %get-tuple-element.19, f32[4096]{0:T(1024)S(1)} %get-tuple-element.20, f32[4096]{0:T(1024)S(1)} %get-tuple-element.18, ...), kind=kLoop, calls=%fused_computation.21 | loop fusion | flops 59768832 | bytes 25247744 | tf_op jit(solution)/shard_map/convert_element_type | solution.py:52
  158.4 3.4 fusion.10
  161.9 3.4 fusion.12
  165.3 3.4 fusion.14
  168.7 3.4 fusion.16
  172.2 0.3 slice_add_fusion
  172.5 0.2 fusion.24
  172.7 0.8 copy.40
  173.5 29.7 %all_to_all.18 = bf16[512,3,2,128]{3,2,1,0:T(2,128)(2,1)S(1)} all-to-all(bf16[512,3,2,128]{3,2,1,0:T(2,128)(2,1)S(1)} %copy.40), channel_id=1, replica_groups=mesh['chan'=32,'stn'=8] {'chan'}, dimensions={0} | all-to-all | bytes 1572864 | tf_op jit(solution)/shard_map/all_to_all | solution.py:81
  203.3 0.1 copy.42
  203.4 1.2 copy.44
  205.1 0.1 reshape.22
  205.4 0.2 copy.48
  205.6 1.2 fusion.59
  206.8 143.1 %all-gather.2.cloned.1.call-done = bf16[16,96,2,1024]{3,1,2,0:T(8,128)(2,1)} async-done(((bf16[16,96,2,128]{3,1,2,0:T(8,128)(2,1)}), bf16[16,96,2,1024]{3,1,2,0:T(8,128)(2,1)}) %all-gather.2.cloned.1.call-update) | async-done | bytes 6291472 | tf_op jit(solution)/shard_map/all_gather | solution.py:85
  350.0 1.3 dynamic-slice_dynamic-update-slice_fusion.4
  351.3 1.3 dynamic-slice_dynamic-update-slice_fusion.3
  352.6 1.3 dynamic-slice_dynamic-update-slice_fusion.2
  353.9 1.3 dynamic-slice_dynamic-update-slice_fusion.1
  355.3 1.3 dynamic-slice_dynamic-update-slice_fusion
  356.6 1.2 convolution_bitcast_fusion.1
  357.9 1.1 convolution_bitcast_fusion
  358.9 3.8 %fusion.1 = bf16[16,2,128,640]{3,2,0,1:T(8,128)(2,1)} fusion(f32[16,1,128,640]{3,2,0,1:T(8,128)S(1)} %convolution_bitcast_fusion, f32[16,1,128,640]{3,2,0,1:T(8,128)S(1)} %convolution_bitcast_fusion.1, f32[128,640]{1,0:T(8,128)S(1)} %copy.48), kind=kLoop, calls=%fused_computation.11 | loop fusion | flops 10485760 | bytes 16056320 | tf_op jit(solution)/shard_map/convert_element_type | solution.py:107
  362.7 5.6 %copy.49 = bf16[16,2,128,640]{3,2,1,0:T(8,128)(2,1)} copy(bf16[16,2,128,640]{3,2,0,1:T(8,128)(2,1)} %fusion.1) | data formatting | bytes 10485760 | tf_op jit(solution)/shard_map/convert_element_type | solution.py:107
  (20 shorter events, 0.7 us)
Async XLA Ops:
  6.5 15.1 %copy-start.1 = (s32[512]{0:T(512)S(1)}, s32[512]{0:T(512)}, u32[]{:S(2)}) copy-start(s32[512]{0:T(512)} %param.4) | copy-start | bytes 6148
  6.5 343.5 %all-gather.2.cloned.1.call-start = ((), (), s32[]{:S(2)}) async-start(), calls=%async_computation.1 | async-start | bytes 7077888 | tf_op jit(solution)/shard_map/all_gather | solution.py:85
  15.2 134.0 %collective-permute-start = (bf16[2,128,3,4096]{1,3,2,0:T(8,128)(2,1)}, bf16[2,128,3,4096]{1,3,2,0:T(8,128)(2,1)}, u32[]{:S(2)}, u32[]{:S(2)}) collective-permute-start(bf16[2,128,3,4096]{1,3,2,0:T(8,128)(2,1)} %bitcast.44), channel_id=1, source_target_pairs={{0,8},{8,16},{16,24},{24,32},{32,40},{40,48},{48,56},{56,64},{64,7... | collective-permute-start | bytes 18874376 | tf_op jit(solution)/shard_map/ppermute | solution.py:15
  53.7 95.5 %slice-start = ((s8[6291456]{0:T(1024)(128)(4,1)}), s8[4194304]{0:T(1024)(128)(4,1)S(1)}, s32[]{:S(2)}) async-start(s8[6291456]{0:T(1024)(128)(4,1)} %bitcast.45), calls=%async_computation.2 | async-start | bytes 8388608
  85.4 63.8 %slice-start.1 = ((s8[6291456]{0:T(1024)(128)(4,1)}), s8[2097152]{0:T(1024)(128)(4,1)S(1)}, s32[]{:S(2)}) async-start(s8[6291456]{0:T(1024)(128)(4,1)} %bitcast.45), calls=%async_computation.3 | async-start | bytes 4194304
  172.5 32.2 %copy-start = (s32[64,512]{1,0:T(8,128)S(1)}, s32[64,512]{1,0:T(8,128)}, u32[]{:S(2)}) copy-start(s32[64,512]{1,0:T(8,128)} %param.5) | copy-start | bytes 393220
Sparse Core Ops, SparseCore 0:
  204.8 145.1 all-gather.1
where the time goes:
time: 376 us; the launch traced here: 375 us
  other arithmetic  143 us (38%)
  waiting for transfers between devices  143 us (38%)
  blocking collectives  29.7 us (8%)
  local copies, waits for them, and re-layouts  23.9 us (6%)
  matrix products  16 us (4%)
  between operations  14.5 us (4%)
  starting transfers between devices  4.5 us (1%)
    all_gather x1, waiting for transfers between devices, on_device(): everyone = lax.all_gather(turned, 'stn', axis=3, tiled=True)  143 us
    dot_general x2, other arithmetic, transform(): lax.dot_general(sine_table, frames, contract, preferred_element_type=jnp....  64 us
    dot_general x2, other arithmetic, transform(): lax.dot_general(cosine, frames, contract, preferred_element_type=jnp.floa...  63.4 us
    all_to_all x1, blocking collectives, on_device(): lax.all_to_all(spectra, 'chan', split_axis=0, concat_axis=1, tiled=True)  29.7 us
    unnamed x13, local copies, waits for them, and re-layouts  13.9 us
    convert_element_type x1, other arithmetic, carry_frames(): return jnp.transpose(carried, (2, 0, 1, 3)).astype(jnp.bfloat16)  9.25 us
  transfers between devices with their start and end apart: 2, of which 1 were waited for; matrix products, arithmetic and copies ran while one was open for 35% of the time, Pallas kernels for 0%

commit v1 on v0

v1 whole, which is shorter than its diff:
```python
import functools
import math

import jax
import jax.numpy as jnp
import numpy as np
from jax import lax
from jax.experimental import pallas as pl
from jax.experimental.pallas import tpu as pltpu
from jax.sharding import PartitionSpec as P

N = 4096
TAPS = 4

def window_np():
    pos = np.arange(TAPS * N, dtype=np.float64) + 0.5
    w = np.sinc(pos / N - TAPS / 2.0) * (0.5 - 0.5 * np.cos(2.0 * np.pi / (TAPS * N) * pos))
    w = w / np.sqrt(np.sum(w * w))
    return w.reshape(TAPS, N).astype(np.float32)

def cos_sin(q):
    quad = (q + 512) // 1024
    r = (q - quad * 1024).astype(jnp.float32) * (2.0 * math.pi / N)
    z = r * r
    s = r + r * z * (-1.0 / 6 + z * (1.0 / 120 + z * (-1.0 / 5040 + z * (1.0 / 362880))))
    c = 1.0 + z * (-0.5 + z * (1.0 / 24 + z * (-1.0 / 720 + z * (1.0 / 40320))))
    quad = quad & 3
    odd = (quad & 1) == 1
    cc = jnp.where(odd, s, c)
    ss = jnp.where(odd, c, s)
    cc = jnp.where((quad == 1) | (quad == 2), -cc, cc)
    ss = jnp.where(quad >= 2, -ss, ss)
    return cc, ss

ROWS = 64
def make_tables(ci_ref, tc_ref, ts_ref, lanes):
    for lc in lanes:
        for half in range(128 // ROWS):
            k = ci_ref[0:1, lc * 128:(lc + 1) * 128]
            k8 = jnp.broadcast_to(k, (8, 128))
            cd, sd = cos_sin((k8 * 128) & (N - 1))
            b = (lax.broadcasted_iota(jnp.int32, (ROWS // 8, 8, 128), 0) * 8
                 + lax.broadcasted_iota(jnp.int32, (ROWS // 8, 8, 128), 1) + half * ROWS)
            c, s = cos_sin((b * k8[None]) & (N - 1))
            def step(i, cs):
                c, s = cs
                row = pl.ds(pl.multiple_of(i * 128 + half * ROWS, ROWS), ROWS)
                tc_ref[row, lc * 128:(lc + 1) * 128] = c.reshape(ROWS, 128).astype(jnp.bfloat16)
                ts_ref[row, lc * 128:(lc + 1) * 128] = s.reshape(ROWS, 128).astype(jnp.bfloat16)
                return c * cd[None] - s * sd[None], s * cd[None] + c * sd[None]
            lax.fori_loop(0, N // 128, step, (c, s), unroll=2)

FT = 32
def make_frames(win_ref, x_ref, f_ref):
    def step(i, _):
        m0 = pl.multiple_of(i * 128, 128)
        w = [win_ref[p:p + 1, pl.ds(m0, 128)] for p in range(4)]
        for r in range(2):
            for a in range(0, 128, FT):
                x = [x_ref[r, a:a + FT, pl.ds(pl.multiple_of(t * N + m0, 128), 128)].astype(jnp.float32) for t in range(3)]
                o = [w[3] * x[0], w[2] * x[0] + w[3] * x[1], w[1] * x[0] + w[2] * x[1] + w[3] * x[2],
                     w[0] * x[0] + w[1] * x[1] + w[2] * x[2], w[0] * x[1] + w[1] * x[2], w[0] * x[2]]
                for u in range(6):
                    f_ref[u, r * 128 + a:r * 128 + a + FT, pl.ds(m0, 128)] = o[u].astype(jnp.bfloat16)
        return 0
    lax.fori_loop(0, N // 128, step, 0)

def dft(f_ref, tc_ref, ts_ref, us, n0, nw):
    l = f_ref[us, :, :].reshape(-1, N) if not isinstance(us, int) else f_ref[us]
    pc = jnp.dot(l, tc_ref[:, n0:n0 + nw], preferred_element_type=jnp.float32)
    ps = jnp.dot(l, ts_ref[:, n0:n0 + nw], preferred_element_type=jnp.float32)
    return pc, ps

def kernel1(NU, NW, ci_ref, win_ref, x_hbm, main_ref, carry_ref, x_ref, f_ref, tc_ref, ts_ref, sem):
    cp = pltpu.make_async_copy(x_hbm, x_ref, sem)
    cp.start()
    make_tables(ci_ref, tc_ref, ts_ref, range(4))
    cp.wait()
    make_frames(win_ref, x_ref, f_ref)
    for n0 in range(0, 512, NW):
        def body(ui, _):
            us = pl.ds(ui * NU, NU)
            pc, ps = dft(f_ref, tc_ref, ts_ref, us, n0, NW)
            pc = pc.reshape(NU, 2, 128, NW); ps = ps.reshape(NU, 2, 128, NW)
            re = pc[:, 0] + ps[:, 1]; im = pc[:, 1] - ps[:, 0]
            @pl.when(ui * NU < 3)
            def _():
                for j in range(NU):
                    main_ref[0, ui * NU + j, :, n0:n0 + NW] = re[j]
                    main_ref[1, ui * NU + j, :, n0:n0 + NW] = im[j]
            @pl.when(ui * NU >= 3)
            def _():
                for j in range(NU):
                    carry_ref[0, ui * NU + j - 3, :, n0:n0 + NW] = re[j].astype(jnp.bfloat16)
                    carry_ref[1, ui * NU + j - 3, :, n0:n0 + NW] = im[j].astype(jnp.bfloat16)
            return 0
        lax.fori_loop(0, 6 // NU, body, 0)

def call1(ci, win, x, NU=1, NW=256):
    V = pl.BlockSpec(memory_space=pltpu.VMEM)
    return pl.pallas_call(
        functools.partial(kernel1, NU, NW),
        out_shape=(jax.ShapeDtypeStruct((2, 3, 128, 512), jnp.float32), jax.ShapeDtypeStruct((2, 3, 128, 512), jnp.bfloat16)),
        in_specs=[V, V, pl.BlockSpec(memory_space=pl.ANY)],
        out_specs=(V, V),
        scratch_shapes=[pltpu.VMEM((2, 128, 3 * N), jnp.bfloat16), pltpu.VMEM((6, 256, N), jnp.bfloat16),
                        pltpu.VMEM((N, 512), jnp.bfloat16), pltpu.VMEM((N, 512), jnp.bfloat16), pltpu.SemaphoreType.DMA],
        compiler_params=pltpu.CompilerParams(vmem_limit_bytes=56 * 2**20),
    )(ci.reshape(1, 512), win, x)
MESH = pl.DeviceIdType.MESH

def signal(sem, dest):
    pl.semaphore_signal(sem, inc=1, device_id=dest, device_id_type=MESH)

def kernel2(main_ref, carry_ref, g_ref, cin_ref, p_ref, send_sem, csend, crecv, zrecv, ysend, yrecv):
    chan, stn = lax.axis_index("chan"), lax.axis_index("stn")
    zl, x, core = chan // 8, (chan // 2) % 4, chan % 2
    zh, y = stn // 4, stn % 4
    z = zh * 4 + zl

    def peer(i):
        dz, dx, dc = i // 8, (i // 2) % 4, i % 2
        zz = (z + dz) % 8
        return (zz % 4) * 8 + ((x + dx) % 4) * 2 + (core + dc) % 2, (zz // 4) * 4 + y

    barrier = pltpu.get_barrier_semaphore()
    def greet(i, _):
        signal(barrier, peer(i))
        return 0
    lax.fori_loop(1, 64, greet, 0)
    def greet_y(d, _):
        signal(barrier, (chan, zh * 4 + (y + d) % 4))
        return 0
    lax.fori_loop(1, 4, greet_y, 0)
    pl.semaphore_wait(barrier, 66)

    def carry_copy(dest):
        return pltpu.make_async_remote_copy(src_ref=carry_ref, dst_ref=cin_ref, send_sem=csend, recv_sem=crecv,
                                            device_id=(dest, stn), device_id_type=MESH)
    @pl.when(chan < 31)
    def _():
        carry_copy(chan + 1).start()
    @pl.when(chan == 0)
    def _():
        cin_ref[...] = jnp.zeros_like(cin_ref)
    @pl.when(chan > 0)
    def _():
        carry_copy(chan).wait_recv()

    for k in range(6):
        full = main_ref[k // 3, k % 3] + cin_ref[k // 3, k % 3].astype(jnp.float32)
        for cb in range(4):
            blk = full[:, cb * 128:(cb + 1) * 128].T.astype(jnp.bfloat16)
            p_ref[cb * 8:(cb + 1) * 8, k * 16:(k + 1) * 16, :] = blk.reshape(8, 16, 128)

    def piece(i):
        c2, s2 = peer(i)
        return pltpu.make_async_remote_copy(
            src_ref=p_ref.at[c2], dst_ref=g_ref.at[4 * jnp.where(s2 == stn, 0, 1), chan],
            send_sem=send_sem, recv_sem=zrecv.at[z], device_id=(c2, s2), device_id_type=MESH)
    own = pltpu.make_async_copy(p_ref.at[chan], g_ref.at[0, chan], zrecv.at[z])
    own.start()
    def send(n, _):
        h = n // 8
        dz = 4 + jnp.where(h % 2 == 0, h // 2, 0 - (h + 1) // 2)
        dz = (4 + (1 - 2 * (h % 2)) * ((h + 1) // 2)) % 8
        piece(dz * 8 + n % 8).start()
        return 0
    lax.fori_loop(0, 56, send, 0)
    def send0(n, _):
        piece(n).start()
        return 0
    lax.fori_loop(1, 8, send0, 0)

    def zwait(j, zg):
        v = g_ref.at[j, pl.ds((zg % 4) * 8, 8)]
        pltpu.make_async_copy(v, v, zrecv.at[zg]).wait()

    def ycopy(d, zz):
        jsrc = jnp.where(y + d < 4, 0, 4)
        return pltpu.make_async_remote_copy(
            src_ref=g_ref.at[jsrc, pl.ds(zz * 8, 8)], dst_ref=g_ref.at[d, pl.ds(zz * 8, 8)],
            send_sem=ysend, recv_sem=yrecv.at[d], device_id=(chan, zh * 4 + (y + d) % 4), device_id_type=MESH)
    def relay(q, _):
        zz = (zl + q) % 4
        zwait(0, zh * 4 + zz)
        zwait(4, (1 - zh) * 4 + zz)
        for d in (2, 1, 3):
            ycopy(d, zz).start()
        return 0
    lax.fori_loop(0, 4, relay, 0)
    for d in (1, 2, 3):
        v = g_ref.at[d]
        pltpu.make_async_copy(v, v, yrecv.at[d]).wait()
    v = g_ref.at[pl.ds(1, 3)]
    pltpu.make_async_copy(v, v, ysend).wait()
    v = p_ref.at[pl.ds(0, 31)]
    w = p_ref
    pltpu.make_async_copy(g_ref.at[pl.ds(0, 2), pl.ds(0, 31)], g_ref.at[pl.ds(0, 2), pl.ds(0, 31)], send_sem).wait()
    pltpu.make_async_copy(p_ref.at[0], p_ref.at[0], send_sem).wait()
    @pl.when(chan < 31)
    def _():
        carry_copy(chan + 1).wait_send()

def call2(main, carry):
    V = pl.BlockSpec(memory_space=pltpu.VMEM)
    D = pltpu.SemaphoreType.DMA
    return pl.pallas_call(
        kernel2, out_shape=jax.ShapeDtypeStruct((5, 32, 96, 128), jnp.bfloat16),
        in_specs=[V, V], out_specs=V,
        scratch_shapes=[pltpu.VMEM((2, 3, 128, 512), jnp.bfloat16), pltpu.VMEM((32, 96, 128), jnp.bfloat16),
                        D, D, D, D((8,)), D, D((4,))],
        compiler_params=pltpu.CompilerParams(collective_id=0, has_side_effects=True, vmem_limit_bytes=40 * 2**20),
    )(main, carry)

def kernel3(g_ref, mask_ref, out_ref, f_ref, y_ref):
    @pl.when(pl.program_id(0) == 0)
    def _():
        for j in range(5):
            def conv(s, _):
                f_ref[pl.ds(pl.multiple_of(s * 96, 96), 96), :] = g_ref[j, s].astype(jnp.float32)
                return 0
            lax.fori_loop(0, 32, conv, 0, unroll=4)
            for c in range(16):
                for k in range(6):
                    y_ref[c, k * 32:(k + 1) * 32, j * 128:(j + 1) * 128] = f_ref[pl.ds(k * 16 + c, 32, stride=96), :].astype(jnp.bfloat16)
    m = mask_ref[...]
    for i in range(4):
        c = pl.program_id(0) * 4 + i
        yv = y_ref[c]
        xv = yv[:, :128]
        sv = jnp.concatenate([xv[96:], -xv[:96]], axis=0)
        ct = (((0,), (0,)), ((), ()))
        out_ref[i, 0] = (lax.dot_general(xv, yv, ct, preferred_element_type=jnp.float32) * m).astype(jnp.bfloat16)
        out_ref[i, 1] = (lax.dot_general(sv, yv, ct, preferred_element_type=jnp.float32) * m).astype(jnp.bfloat16)

def call3(g, mask):
    return pl.pallas_call(
        kernel3, grid=(4,), out_shape=jax.ShapeDtypeStruct((16, 2, 128, 640), jnp.bfloat16),
        in_specs=[pl.BlockSpec((5, 32, 96, 128), lambda i: (0, 0, 0, 0)), pl.BlockSpec((128, 640), lambda i: (0, 0))],
        out_specs=pl.BlockSpec((4, 2, 128, 640), lambda i: (i, 0, 0, 0)),
        scratch_shapes=[pltpu.VMEM((32 * 96, 128), jnp.float32), pltpu.VMEM((16, 192, 640), jnp.bfloat16)],
        compiler_params=pltpu.CompilerParams(vmem_limit_bytes=40 * 2**20),
    )(g, mask)
def keep(flags):
    own = lax.axis_index("stn")
    strips = [lax.dynamic_slice_in_dim(flags, (own - o + 8) % 8 * 64, 64, 1) for o in range(5)]
    m = (1 - jnp.concatenate(strips, axis=1)).astype(jnp.float32) / 96
    return jnp.repeat(jnp.repeat(m, 2, axis=0), 2, axis=1)
def on_device(samples, chan_index, flags):
    main, carry = call1(chan_index, jnp.asarray(window_np()), samples, 3, 256)
    g = call2(main, carry)
    return call3(g, keep(flags))
def solution(mesh):
    return jax.shard_map(on_device, mesh=mesh, in_specs=(P(None, "stn", "chan"), P(), P("stn", None)), out_specs=P("chan", None, "stn", None), check_vma=False)
```

time: 376 us -> 120 us (0.32)
  the two profiles are of different devices: /device:TPU:1 before, /device:TPU:39 now
where the time goes in v1:
time: 120 us
  Pallas kernels  116 us (97%)
  local copies, waits for them, and re-layouts  4.17 us (3%)
    pallas_call x1, Pallas kernels, call2(): pl.pallas_call(kernel2, out_shape=jax.ShapeDtypeStruct((5, 32, 96, 128),...  82.5 us
    pallas_call x1, Pallas kernels, call1(): pl.pallas_call(functools.partial(kernel1, NU, NW), out_shape=(jax.ShapeDt...  24 us
    pallas_call x1, Pallas kernels, call3(): pl.pallas_call(kernel3, grid=(4,), out_shape=jax.ShapeDtypeStruct((16, 2,...  9.22 us
    unnamed x4, local copies, waits for them, and re-layouts  2.54 us

profile of v1, /device:TPU:39, one launch (start us, length us, event | category | flops | bytes accessed | tf_op | source)
XLA Modules:
  0.0 120.0 jit_solution(10094806557944247180)
XLA Ops:
  0.0 0.9 constant_dynamic-slice_fusion
  1.0 0.1 concatenate.3
  1.1 0.1 broadcast_in_dim.6
  1.2 0.1 reshape.10
  1.3 0.1 copy.5
  1.4 0.1 broadcast_in_dim.7
  1.5 0.2 copy.6.mask_ref
  1.7 24.0 %shard_map.46 = (f32[2,3,128,512]{3,2,1,0:T(8,128)}, bf16[2,3,128,512]{3,2,1,0:T(8,128)(2,1)}) custom-call(s32[1,512]{1,0:T(1,128)} %bitcast.3, f32[4,4096]{1,0:T(4,128)} %constant.60.clone.win_ref, bf16[2,128,12288]{2,1,0:T(8,128)(2,1)} %x_hbm.1), custom_call_target="tpu_custom_call" | custom-call | tf_op jit(solution)/shard_map/pallas_call | solution.py:101
  25.7 0.0 copy-start
  25.7 1.4 %copy-done = f32[2,3,128,512]{3,2,1,0:T(8,128)S(1)} copy-done((f32[2,3,128,512]{3,2,1,0:T(8,128)S(1)}, f32[2,3,128,512]{3,2,1,0:T(8,128)}, u32[]{:S(2)}) %copy-start) | copy-done | bytes 1572888
  27.1 0.0 copy-start.1
  27.1 1.1 copy-done.1
  28.3 82.5 %shard_map.47.g_ref = bf16[5,32,96,128]{3,2,1,0:T(8,128)(2,1)S(1)} custom-call(f32[2,3,128,512]{3,2,1,0:T(8,128)S(1)} %copy-done, bf16[2,3,128,512]{3,2,1,0:T(8,128)(2,1)S(1)} %copy-done.1), custom_call_target="tpu_custom_call" | custom-call | tf_op jit(solution)/shard_map/pallas_call | solution.py:208
  110.8 9.2 %shard_map.48 = bf16[16,2,128,640]{3,2,1,0:T(8,128)(2,1)} custom-call(bf16[5,32,96,128]{3,2,1,0:T(8,128)(2,1)S(1)} %shard_map.47.g_ref, f32[128,640]{1,0:T(8,128)S(1)} %copy.6.mask_ref), custom_call_target="tpu_custom_call" | custom-call | tf_op jit(solution)/shard_map/pallas_call | solution.py:238
  (1 shorter events, 0.0 us)
Async XLA Ops:
  25.7 1.4 %copy-start = (f32[2,3,128,512]{3,2,1,0:T(8,128)S(1)}, f32[2,3,128,512]{3,2,1,0:T(8,128)}, u32[]{:S(2)}) copy-start(f32[2,3,128,512]{3,2,1,0:T(8,128)} %get-tuple-element.7.main_ref) | copy-start | bytes 4718596
  27.1 1.1 copy-start.1

commit v2 on v1

v2 whole, which is shorter than its diff:
```python
import functools
import math

import jax
import jax.numpy as jnp
import numpy as np
from jax import lax
from jax.experimental import pallas as pl
from jax.experimental.pallas import tpu as pltpu
from jax.sharding import PartitionSpec as P

N = 4096
TAPS = 4

def window_np():
    pos = np.arange(TAPS * N, dtype=np.float64) + 0.5
    w = np.sinc(pos / N - TAPS / 2.0) * (0.5 - 0.5 * np.cos(2.0 * np.pi / (TAPS * N) * pos))
    w = w / np.sqrt(np.sum(w * w))
    return w.reshape(TAPS, N).astype(np.float32)

def cos_sin(q):
    quad = (q + 512) // 1024
    r = (q - quad * 1024).astype(jnp.float32) * (2.0 * math.pi / N)
    z = r * r
    s = r + r * z * (-1.0 / 6 + z * (1.0 / 120 + z * (-1.0 / 5040 + z * (1.0 / 362880))))
    c = 1.0 + z * (-0.5 + z * (1.0 / 24 + z * (-1.0 / 720 + z * (1.0 / 40320))))
    quad = quad & 3
    odd = (quad & 1) == 1
    cc = jnp.where(odd, s, c)
    ss = jnp.where(odd, c, s)
    cc = jnp.where((quad == 1) | (quad == 2), -cc, cc)
    ss = jnp.where(quad >= 2, -ss, ss)
    return cc, ss

ROWS = 64
def make_tables(ci_ref, tc_ref, ts_ref, lanes):
    for lc in lanes:
        for half in range(128 // ROWS):
            k = ci_ref[0:1, lc * 128:(lc + 1) * 128]
            k8 = jnp.broadcast_to(k, (8, 128))
            cd, sd = cos_sin((k8 * 128) & (N - 1))
            b = (lax.broadcasted_iota(jnp.int32, (ROWS // 8, 8, 128), 0) * 8
                 + lax.broadcasted_iota(jnp.int32, (ROWS // 8, 8, 128), 1) + half * ROWS)
            c, s = cos_sin((b * k8[None]) & (N - 1))
            def step(i, cs):
                c, s = cs
                row = pl.ds(pl.multiple_of(i * 128 + half * ROWS, ROWS), ROWS)
                tc_ref[row, lc * 128:(lc + 1) * 128] = c.reshape(ROWS, 128).astype(jnp.bfloat16)
                ts_ref[row, lc * 128:(lc + 1) * 128] = s.reshape(ROWS, 128).astype(jnp.bfloat16)
                return c * cd[None] - s * sd[None], s * cd[None] + c * sd[None]
            lax.fori_loop(0, N // 128, step, (c, s), unroll=2)

FT = 32
MESH = pl.DeviceIdType.MESH
UNITS = (2, 1, 0)

def signal(sem, dest):
    pl.semaphore_signal(sem, inc=1, device_id=dest, device_id_type=MESH)

def make_unit_frames(u, win_ref, x_ref, f_ref):
    def step(i, _):
        m0 = pl.multiple_of(i * 128, 128)
        w = [win_ref[p:p + 1, pl.ds(m0, 128)] for p in range(4)]
        for r in range(2):
            for a in range(0, 128, FT):
                x = [x_ref[r, a:a + FT, pl.ds(pl.multiple_of(t * N + m0, 128), 128)].astype(jnp.float32) for t in range(3)]
                cur = sum(w[3 - u + t] * x[t] for t in range(u + 1))
                car = sum(w[t - u] * x[t] for t in range(u, 3))
                row = slice(r * 128 + a, r * 128 + a + FT)
                f_ref[0, row, pl.ds(m0, 128)] = car.astype(jnp.bfloat16)
                f_ref[1, row, pl.ds(m0, 128)] = cur.astype(jnp.bfloat16)
        return 0
    lax.fori_loop(0, N // 128, step, 0)

def half_dft(frame, tc_ref, ts_ref, n0, nw):
    pc = jnp.dot(frame, tc_ref[:, n0:n0 + nw], preferred_element_type=jnp.float32)
    ps = jnp.dot(frame, ts_ref[:, n0:n0 + nw], preferred_element_type=jnp.float32)
    return pc[:128] + ps[128:], pc[128:] - ps[:128]

def exchange_kernel(ci_ref, win_ref, x_hbm, g_ref, x_ref, f_ref, tc_ref, ts_ref, main_ref, cout_ref, cin_ref, p_ref,
                    xsem, csend, crecv, zsend, zrecv, ysend, yrecv):
    chan, stn = lax.axis_index("chan"), lax.axis_index("stn")
    zl, x, core = chan // 8, (chan // 2) % 4, chan % 2
    zh, y = stn // 4, stn % 4
    late = y // 2

    xcopy = pltpu.make_async_copy(x_hbm, x_ref, xsem)
    xcopy.start()

    barrier = pltpu.get_barrier_semaphore()
    def peer(n):
        far = (n // 32 + late) % 2
        q = (n // 8) % 4
        zz = (zl + 4 - q) % 4
        return zz * 8 + ((x + (n // 2) % 4) % 4) * 2 + (core + n) % 2, ((zh + far) % 2) * 4 + y, far
    def greet(n, _):
        c2, s2, far = peer(n)
        @pl.when(jnp.logical_or(c2 != chan, s2 != stn))
        def _():
            signal(barrier, (c2, s2))
        return 0
    lax.fori_loop(0, 64, greet, 0)
    def greet_y(d, _):
        signal(barrier, (chan, zh * 4 + (y + d) % 4))
        return 0
    lax.fori_loop(1, 4, greet_y, 0)

    make_tables(ci_ref, tc_ref, ts_ref, range(4))
    xcopy.wait()

    def carry_copy(u, dest):
        return pltpu.make_async_remote_copy(src_ref=cout_ref.at[u], dst_ref=cin_ref.at[u], send_sem=csend.at[u],
                                            recv_sem=crecv.at[u], device_id=(dest, stn), device_id_type=MESH)

    def send_pieces(u):
        pltpu.make_async_copy(p_ref.at[u, chan], g_ref.at[0, u, chan], zrecv.at[u, zh * 4 + zl]).start()
        def send(n, _):
            c2, s2, far = peer(n)
            @pl.when(jnp.logical_or(c2 != chan, s2 != stn))
            def _():
                pltpu.make_async_remote_copy(
                    src_ref=p_ref.at[u, c2], dst_ref=g_ref.at[4 * far, u, chan], send_sem=zsend,
                    recv_sem=zrecv.at[u, zh * 4 + zl], device_id=(c2, s2), device_id_type=MESH).start()
            return 0
        lax.fori_loop(0, 64, send, 0)

    def forward(u, first, last):
        def group(n, _):
            far = (n // 4 + late) % 2
            zz = (zl + n) % 4
            v = g_ref.at[4 * far, u, pl.ds(zz * 8, 8)]
            pltpu.make_async_copy(v, v, zrecv.at[u, ((zh + far) % 2) * 4 + zz]).wait()
            for d in (2, 1, 3):
                @pl.when((y + d) // 4 == far)
                def _():
                    pltpu.make_async_remote_copy(
                        src_ref=g_ref.at[4 * far, u, pl.ds(zz * 8, 8)], dst_ref=g_ref.at[d, u, pl.ds(zz * 8, 8)],
                        send_sem=ysend, recv_sem=yrecv.at[u], device_id=(chan, zh * 4 + (y + d) % 4),
                        device_id_type=MESH).start()
            return 0
        lax.fori_loop(first, last, group, 0)

    for i, u in enumerate(UNITS):
        make_unit_frames(u, win_ref, x_ref, f_ref)
        for n0 in range(0, 512, NW):
            re, im = half_dft(f_ref[0], tc_ref, ts_ref, n0, NW)
            cout_ref[u, 0, :, n0:n0 + NW] = re.astype(jnp.bfloat16)
            cout_ref[u, 1, :, n0:n0 + NW] = im.astype(jnp.bfloat16)
        if i == 0:
            pl.semaphore_wait(barrier, 66)
        @pl.when(chan < 31)
        def _():
            carry_copy(u, chan + 1).start()
        for n0 in range(0, 512, NW):
            re, im = half_dft(f_ref[1], tc_ref, ts_ref, n0, NW)
            main_ref[0, :, n0:n0 + NW] = re
            main_ref[1, :, n0:n0 + NW] = im
        @pl.when(chan == 0)
        def _():
            cin_ref[u] = jnp.zeros((2, 128, 512), jnp.bfloat16)
        @pl.when(chan > 0)
        def _():
            carry_copy(u, chan).wait_recv()
        for r in range(2):
            full = main_ref[r] + cin_ref[u, r].astype(jnp.float32)
            for cb in range(4):
                blk = full[:, cb * 128:(cb + 1) * 128].T.astype(jnp.bfloat16)
                p_ref[u, cb * 8:(cb + 1) * 8, r * 16:(r + 1) * 16, :] = blk.reshape(8, 16, 128)
        send_pieces(u)
        if i == 1:
            forward(UNITS[0], 0, 4)
    forward(UNITS[0], 4, 8)
    forward(UNITS[1], 0, 8)
    forward(UNITS[2], 0, 8)
    for u in UNITS:
        v = g_ref.at[pl.ds(1, 3), u]
        pltpu.make_async_copy(v, v, yrecv.at[u]).wait()
    for u in UNITS:
        v = g_ref.at[pl.ds(1, 3), u]
        pltpu.make_async_copy(v, v, ysend).wait()
        v = g_ref.at[pl.ds(0, 2), u, pl.ds(0, 31)]
        pltpu.make_async_copy(v, v, zsend).wait()
        v = p_ref.at[u, 0]
        pltpu.make_async_copy(v, v, zsend).wait()
        @pl.when(chan < 31)
        def _():
            carry_copy(u, chan + 1).wait_send()

NW = 256
def exchange(ci, win, x):
    V = pl.BlockSpec(memory_space=pltpu.VMEM)
    D = pltpu.SemaphoreType.DMA
    bf = jnp.bfloat16
    return pl.pallas_call(
        exchange_kernel, out_shape=jax.ShapeDtypeStruct((5, 3, 32, 32, 128), bf),
        in_specs=[V, V, pl.BlockSpec(memory_space=pl.ANY)], out_specs=V,
        scratch_shapes=[pltpu.VMEM((2, 128, 3 * N), bf), pltpu.VMEM((2, 256, N), bf), pltpu.VMEM((N, 512), bf), pltpu.VMEM((N, 512), bf),
                        pltpu.VMEM((2, 128, 512), jnp.float32), pltpu.VMEM((3, 2, 128, 512), bf), pltpu.VMEM((3, 2, 128, 512), bf),
                        pltpu.VMEM((3, 32, 32, 128), bf),
                        D, D((3,)), D((3,)), D, D((3, 8)), D, D((3,))],
        compiler_params=pltpu.CompilerParams(collective_id=0, has_side_effects=True, vmem_limit_bytes=52 * 2**20),
    )(ci.reshape(1, 512), win, x)

def correlate_kernel(g_ref, mask_ref, out_ref, gv_ref, f_ref, y_ref, sem):
    @pl.when(pl.program_id(0) == 0)
    def _():
        copies = [pltpu.make_async_copy(g_ref.at[j], gv_ref.at[j], sem.at[j]) for j in range(5)]
        for c in copies:
            c.start()
        for j in range(5):
            copies[j].wait()
            for u in range(3):
                f_ref[u * 1024:(u + 1) * 1024, :] = gv_ref[j, u].reshape(1024, 128).astype(jnp.float32)
            for c in range(16):
                for r in range(2):
                    for u in range(3):
                        k = r * 3 + u
                        y_ref[c, k * 32:(k + 1) * 32, j * 128:(j + 1) * 128] = (
                            f_ref[pl.ds(u * 1024 + r * 16 + c, 32, stride=32), :].astype(jnp.bfloat16))
    m = mask_ref[...]
    for i in range(4):
        c = pl.program_id(0) * 4 + i
        yv = y_ref[c]
        xv = yv[:, :128]
        sv = jnp.concatenate([xv[96:], -xv[:96]], axis=0)
        ct = (((0,), (0,)), ((), ()))
        out_ref[i, 0] = (lax.dot_general(xv, yv, ct, preferred_element_type=jnp.float32) * m).astype(jnp.bfloat16)
        out_ref[i, 1] = (lax.dot_general(sv, yv, ct, preferred_element_type=jnp.float32) * m).astype(jnp.bfloat16)

def correlate(g, mask):
    return pl.pallas_call(
        correlate_kernel, grid=(4,), out_shape=jax.ShapeDtypeStruct((16, 2, 128, 640), jnp.bfloat16),
        in_specs=[pl.BlockSpec(memory_space=pl.ANY), pl.BlockSpec((128, 640), lambda i: (0, 0))],
        out_specs=pl.BlockSpec((4, 2, 128, 640), lambda i: (i, 0, 0, 0)),
        scratch_shapes=[pltpu.VMEM((5, 3, 32, 32, 128), jnp.bfloat16), pltpu.VMEM((3072, 128), jnp.float32),
                        pltpu.VMEM((16, 192, 640), jnp.bfloat16), pltpu.SemaphoreType.DMA((5,))],
        compiler_params=pltpu.CompilerParams(vmem_limit_bytes=40 * 2**20),
    )(g, mask)
def keep_factor(flags):
    own = lax.axis_index("stn")
    strips = [lax.dynamic_slice_in_dim(flags, (own - o + 8) % 8 * 64, 64, 1) for o in range(5)]
    m = (1 - jnp.concatenate(strips, axis=1)).astype(jnp.float32) / 96
    return jnp.repeat(jnp.repeat(m, 2, axis=0), 2, axis=1)

def on_device(samples, chan_index, flags):
    g = exchange(chan_index, jnp.asarray(window_np()), samples)
    return correlate(g, keep_factor(flags))

def solution(mesh):
    return jax.shard_map(on_device, mesh=mesh, in_specs=(P(None, "stn", "chan"), P(), P("stn", None)),
                         out_specs=P("chan", None, "stn", None), check_vma=False)
```

time: 120 us -> 96.1 us (0.80)
  the two profiles are of different devices: /device:TPU:39 before, /device:TPU:1 now
where the time goes in v2:
time: 96.1 us; the launch traced here: 94.4 us
  Pallas kernels  88.9 us (93%)
  local copies, waits for them, and re-layouts  5.24 us (5%)
    pallas_call x1, Pallas kernels, exchange(): pl.pallas_call(exchange_kernel, out_shape=jax.ShapeDtypeStruct((5, 3, 32,...  78.6 us
    pallas_call x1, Pallas kernels, correlate(): pl.pallas_call(correlate_kernel, grid=(4,), out_shape=jax.ShapeDtypeStruc...  10.3 us
    unnamed x6, local copies, waits for them, and re-layouts  3.63 us

profile of v2, /device:TPU:1, one launch (start us, length us, event | category | flops | bytes accessed | tf_op | source)
XLA Modules:
  0.0 94.4 jit_solution(13779973160130467295)
XLA Ops:
  0.0 0.9 constant_dynamic-slice_fusion
  0.9 0.1 concatenate.3
  1.1 0.1 broadcast_in_dim.6
  1.1 0.1 reshape.10
  1.3 0.1 copy.5
  1.4 0.1 broadcast_in_dim.7
  1.5 0.2 copy.6.mask_ref
  1.7 0.0 copy-start.1
  1.7 0.8 copy-done.1
  2.5 0.0 copy-start.2
  2.5 0.7 copy-done.2
  3.2 78.6 %shard_map.46.g_ref = bf16[5,3,32,32,128]{4,3,2,1,0:T(8,128)(2,1)} custom-call(s32[1,512]{1,0:T(1,128)S(1)} %bitcast.2, f32[4,4096]{1,0:T(4,128)S(1)} %copy-done.1, bf16[2,128,12288]{2,1,0:T(8,128)(2,1)} %x_hbm.1), custom_call_target="tpu_custom_call" | custom-call | tf_op jit(solution)/shard_map/pallas_call | solution.py:194
  81.9 0.0 copy-start
  81.9 2.1 %copy-done = bf16[5,3,32,32,128]{4,3,2,1,0:T(8,128)(2,1)S(1)} copy-done((bf16[5,3,32,32,128]{4,3,2,1,0:T(8,128)(2,1)S(1)}, bf16[5,3,32,32,128]{4,3,2,1,0:T(8,128)(2,1)}, u32[]{:S(2)}) %copy-start) | copy-done | bytes 3932184
  84.0 10.3 %shard_map.47 = bf16[16,2,128,640]{3,2,1,0:T(8,128)(2,1)} custom-call(bf16[5,3,32,32,128]{4,3,2,1,0:T(8,128)(2,1)S(1)} %copy-done, f32[128,640]{1,0:T(8,128)S(1)} %copy.6.mask_ref), custom_call_target="tpu_custom_call" | custom-call | tf_op jit(solution)/shard_map/pallas_call | solution.py:231
  (1 shorter events, 0.0 us)
Async XLA Ops:
  1.7 0.8 copy-start.1
  2.5 0.7 copy-start.2
  81.9 2.1 %copy-start = (bf16[5,3,32,32,128]{4,3,2,1,0:T(8,128)(2,1)S(1)}, bf16[5,3,32,32,128]{4,3,2,1,0:T(8,128)(2,1)}, u32[]{:S(2)}) copy-start(bf16[5,3,32,32,128]{4,3,2,1,0:T(8,128)(2,1)} %shard_map.46.g_ref) | copy-start | bytes 11796484

commit v3 on v2

v3 whole, which is shorter than its diff:
```python
import functools
import math

import jax
import jax.numpy as jnp
import numpy as np
from jax import lax
from jax.experimental import pallas as pl
from jax.experimental.pallas import tpu as pltpu
from jax.sharding import PartitionSpec as P

N = 4096
TAPS = 4

def window_np():
    pos = np.arange(TAPS * N, dtype=np.float64) + 0.5
    w = np.sinc(pos / N - TAPS / 2.0) * (0.5 - 0.5 * np.cos(2.0 * np.pi / (TAPS * N) * pos))
    w = w / np.sqrt(np.sum(w * w))
    return w.reshape(TAPS, N).astype(np.float32)

def cos_sin(q):
    quad = (q + 512) // 1024
    r = (q - quad * 1024).astype(jnp.float32) * (2.0 * math.pi / N)
    z = r * r
    s = r + r * z * (-1.0 / 6 + z * (1.0 / 120 + z * (-1.0 / 5040 + z * (1.0 / 362880))))
    c = 1.0 + z * (-0.5 + z * (1.0 / 24 + z * (-1.0 / 720 + z * (1.0 / 40320))))
    quad = quad & 3
    odd = (quad & 1) == 1
    cc = jnp.where(odd, s, c)
    ss = jnp.where(odd, c, s)
    cc = jnp.where((quad == 1) | (quad == 2), -cc, cc)
    ss = jnp.where(quad >= 2, -ss, ss)
    return cc, ss

ROWS = 64
def make_tables(ci_ref, tc_ref, ts_ref, lanes):
    for lc in lanes:
        for half in range(128 // ROWS):
            k = ci_ref[0:1, lc * 128:(lc + 1) * 128]
            k8 = jnp.broadcast_to(k, (8, 128))
            cd, sd = cos_sin((k8 * 128) & (N - 1))
            b = (lax.broadcasted_iota(jnp.int32, (ROWS // 8, 8, 128), 0) * 8
                 + lax.broadcasted_iota(jnp.int32, (ROWS // 8, 8, 128), 1) + half * ROWS)
            c, s = cos_sin((b * k8[None]) & (N - 1))
            def step(i, cs):
                c, s = cs
                row = pl.ds(pl.multiple_of(i * 128 + half * ROWS, ROWS), ROWS)
                tc_ref[row, lc * 128:(lc + 1) * 128] = c.reshape(ROWS, 128).astype(jnp.bfloat16)
                ts_ref[row, lc * 128:(lc + 1) * 128] = s.reshape(ROWS, 128).astype(jnp.bfloat16)
                return c * cd[None] - s * sd[None], s * cd[None] + c * sd[None]
            lax.fori_loop(0, N // 128, step, (c, s), unroll=2)

FT = 32
MESH = pl.DeviceIdType.MESH
UNITS = (2, 1, 0)

def signal(sem, dest):
    pl.semaphore_signal(sem, inc=1, device_id=dest, device_id_type=MESH)

def make_frames(u, carried, win_ref, x_ref, f_ref):
    def step(i, _):
        m0 = pl.multiple_of(i * 128, 128)
        w = [win_ref[p:p + 1, pl.ds(m0, 128)] for p in range(4)]
        segments = range(u, 3) if carried else range(u + 1)
        for r in range(2):
            for a in range(0, 128, FT):
                frame = 0.0
                for t in segments:
                    x = x_ref[r, a:a + FT, pl.ds(pl.multiple_of(t * N + m0, 128), 128)].astype(jnp.float32)
                    frame = frame + w[t - u if carried else 3 - u + t] * x
                f_ref[r * 128 + a:r * 128 + a + FT, pl.ds(m0, 128)] = frame.astype(jnp.bfloat16)
        return 0
    lax.fori_loop(0, N // 128, step, 0)

def relayout(j, u, g_ref, wide_ref, y_ref):
    lanes = pl.ds(pl.multiple_of(j * 128, 128), 128)
    wide_ref[...] = g_ref[j, u].reshape(1024, 128).astype(jnp.float32)
    for c in range(16):
        for r in range(2):
            k = (r * 3 + u) * 32
            y_ref[c, k:k + 32, lanes] = wide_ref[pl.ds(r * 16 + c, 32, stride=32), :].astype(jnp.bfloat16)

def half_dft(frame, tc_ref, ts_ref, n0, nw):
    pc = jnp.dot(frame, tc_ref[:, n0:n0 + nw], preferred_element_type=jnp.float32)
    ps = jnp.dot(frame, ts_ref[:, n0:n0 + nw], preferred_element_type=jnp.float32)
    return pc[:128] + ps[128:], pc[128:] - ps[:128]

def exchange_kernel(ci_ref, win_hbm, x_hbm, y_ref, g_ref, wide_ref, win_ref, x_ref, f_ref, tc_ref, ts_ref, main_ref, cout_ref, cin_ref, p_ref,
                    xsem, wsem, csend, crecv, zsend, zrecv, ysend, yrecv):
    chan, stn = lax.axis_index("chan"), lax.axis_index("stn")
    zl, x, core = chan // 8, (chan // 2) % 4, chan % 2
    zh, y = stn // 4, stn % 4
    late = y // 2

    xcopy = pltpu.make_async_copy(x_hbm, x_ref, xsem)
    xcopy.start()
    wcopy = pltpu.make_async_copy(win_hbm, win_ref, wsem)
    wcopy.start()

    barrier = pltpu.get_barrier_semaphore()
    def peer(n):
        far = (n // 32 + late) % 2
        q = (n // 8) % 4
        zz = (zl + 4 - q) % 4
        return zz * 8 + ((x + (n // 2) % 4) % 4) * 2 + (core + n) % 2, ((zh + far) % 2) * 4 + y, far
    def greet(n, _):
        c2, s2, far = peer(n)
        @pl.when(jnp.logical_or(c2 != chan, s2 != stn))
        def _():
            signal(barrier, (c2, s2))
        return 0
    lax.fori_loop(0, 64, greet, 0)
    def greet_y(d, _):
        signal(barrier, (chan, zh * 4 + (y + d) % 4))
        return 0
    lax.fori_loop(1, 4, greet_y, 0)

    make_tables(ci_ref, tc_ref, ts_ref, range(4))
    wcopy.wait()
    xcopy.wait()

    def carry_copy(u, dest):
        return pltpu.make_async_remote_copy(src_ref=cout_ref.at[u], dst_ref=cin_ref.at[u], send_sem=csend.at[u],
                                            recv_sem=crecv.at[u], device_id=(dest, stn), device_id_type=MESH)

    def keep_own(u):
        pltpu.make_async_copy(p_ref.at[u, chan], g_ref.at[0, u, chan], zrecv.at[u, zh * 4 + zl]).start()

    def send_batch(u, b):
        def send(n, _):
            c2, s2, far = peer(n)
            @pl.when(jnp.logical_or(c2 != chan, s2 != stn))
            def _():
                pltpu.make_async_remote_copy(
                    src_ref=p_ref.at[u, c2], dst_ref=g_ref.at[4 * far, u, chan], send_sem=zsend,
                    recv_sem=zrecv.at[u, zh * 4 + zl], device_id=(c2, s2), device_id_type=MESH).start()
            return 0
        lax.fori_loop(b * 8, b * 8 + 8, send, 0)

    def forward(u, n):
        far = (n // 4 + late) % 2
        zz = (zl + n) % 4
        v = g_ref.at[4 * far, u, pl.ds(zz * 8, 8)]
        pltpu.make_async_copy(v, v, zrecv.at[u, ((zh + far) % 2) * 4 + zz]).wait()
        for d in (2, 1, 3):
            @pl.when((y + d) // 4 == far)
            def _():
                pltpu.make_async_remote_copy(
                    src_ref=g_ref.at[4 * far, u, pl.ds(zz * 8, 8)], dst_ref=g_ref.at[d, u, pl.ds(zz * 8, 8)],
                    send_sem=ysend, recv_sem=yrecv.at[u], device_id=(chan, zh * 4 + (y + d) % 4),
                    device_id_type=MESH).start()

    def carried_part(u):
        make_frames(u, True, win_ref, x_ref, f_ref)
        for n0 in range(0, 512, NW):
            re, im = half_dft(f_ref[...], tc_ref, ts_ref, n0, NW)
            cout_ref[u, 0, :, n0:n0 + NW] = re.astype(jnp.bfloat16)
            cout_ref[u, 1, :, n0:n0 + NW] = im.astype(jnp.bfloat16)
        if u == UNITS[0]:
            pl.semaphore_wait(barrier, 66)
        @pl.when(chan < 31)
        def _():
            carry_copy(u, chan + 1).start()

    def current_part(u):
        make_frames(u, False, win_ref, x_ref, f_ref)
        for n0 in range(0, 512, NW):
            re, im = half_dft(f_ref[...], tc_ref, ts_ref, n0, NW)
            main_ref[0, :, n0:n0 + NW] = re
            main_ref[1, :, n0:n0 + NW] = im

    def pieces(u):
        @pl.when(chan == 0)
        def _():
            cin_ref[u] = jnp.zeros((2, 128, 512), jnp.bfloat16)
        @pl.when(chan > 0)
        def _():
            carry_copy(u, chan).wait_recv()
        for r in range(2):
            full = main_ref[r] + cin_ref[u, r].astype(jnp.float32)
            for cb in range(4):
                blk = full[:, cb * 128:(cb + 1) * 128].T.astype(jnp.bfloat16)
                p_ref[u, cb * 8:(cb + 1) * 8, r * 16:(r + 1) * 16, :] = blk.reshape(8, 16, 128)
        keep_own(u)

    def own_blocks(u):
        relayout(0, u, g_ref, wide_ref, y_ref)
        relayout(4, u, g_ref, wide_ref, y_ref)

    def other_blocks(u):
        v = g_ref.at[pl.ds(1, 3), u]
        pltpu.make_async_copy(v, v, yrecv.at[u]).wait()
        for j in range(1, 4):
            relayout(j, u, g_ref, wide_ref, y_ref)

    def steps(before, after, start, stop):
        def step(n, _):
            if before is not None:
                forward(before, n)
            if after is not None:
                send_batch(after, n)
            return 0
        lax.fori_loop(start, stop, step, 0)

    first, second, third = UNITS
    carried_part(first)
    current_part(first)
    pieces(first)
    steps(None, first, 0, 4)
    carried_part(second)
    steps(None, first, 4, 8)
    current_part(second)
    steps(first, None, 0, 3)
    carried_part(third)
    steps(first, None, 3, 5)
    pieces(second)
    steps(None, second, 0, 4)
    current_part(third)
    steps(first, None, 5, 6)
    steps(first, second, 6, 8)
    steps(None, second, 4, 6)
    pieces(third)
    steps(second, third, 0, 8)
    own_blocks(first)
    own_blocks(second)
    steps(third, None, 0, 8)
    other_blocks(first)
    own_blocks(third)
    other_blocks(second)
    other_blocks(third)
    for u in UNITS:
        v = g_ref.at[pl.ds(1, 3), u]
        pltpu.make_async_copy(v, v, ysend).wait()
        v = g_ref.at[pl.ds(0, 2), u, pl.ds(0, 31)]
        pltpu.make_async_copy(v, v, zsend).wait()
        v = p_ref.at[u, 0]
        pltpu.make_async_copy(v, v, zsend).wait()
        @pl.when(chan < 31)
        def _():
            carry_copy(u, chan + 1).wait_send()

NW = 256
def exchange(ci, win, x):
    V = pl.BlockSpec(memory_space=pltpu.VMEM)
    D = pltpu.SemaphoreType.DMA
    bf = jnp.bfloat16
    return pl.pallas_call(
        exchange_kernel, out_shape=jax.ShapeDtypeStruct((16, 192, 640), bf),
        in_specs=[V, pl.BlockSpec(memory_space=pl.ANY), pl.BlockSpec(memory_space=pl.ANY)], out_specs=V,
        scratch_shapes=[pltpu.VMEM((5, 3, 32, 32, 128), bf), pltpu.VMEM((1024, 128), jnp.float32), pltpu.VMEM((TAPS, N), jnp.float32),
                        pltpu.VMEM((2, 128, 3 * N), bf), pltpu.VMEM((256, N), bf), pltpu.VMEM((N, 512), bf), pltpu.VMEM((N, 512), bf),
                        pltpu.VMEM((2, 128, 512), jnp.float32), pltpu.VMEM((3, 2, 128, 512), bf), pltpu.VMEM((3, 2, 128, 512), bf),
                        pltpu.VMEM((3, 32, 32, 128), bf),
                        D, D, D((3,)), D((3,)), D, D((3, 8)), D, D((3,))],
        compiler_params=pltpu.CompilerParams(collective_id=0, has_side_effects=True, vmem_limit_bytes=58 * 2**20),
    )(ci.reshape(1, 512), win, x)

def keep_factor(flags_ref, keep_ref):
    own = lax.axis_index("stn")
    kept = (1 - flags_ref[...]).astype(jnp.float32).astype(jnp.bfloat16)
    pair = lax.broadcasted_iota(jnp.int32, (128, 64), 0) // 2 == lax.broadcasted_iota(jnp.int32, (128, 64), 1)
    pair = pair.astype(jnp.float32).astype(jnp.bfloat16)
    station = lax.broadcasted_iota(jnp.int32, (512, 128), 1) // 2
    for j in range(5):
        pick = lax.broadcasted_iota(jnp.int32, (512, 128), 0) == station + (own + 8 - j) % 8 * 64
        strip = jnp.dot(kept, pick.astype(jnp.float32).astype(jnp.bfloat16), preferred_element_type=jnp.float32)
        full = jnp.dot(pair, strip.astype(jnp.bfloat16), preferred_element_type=jnp.float32)
        keep_ref[:, j * 128:(j + 1) * 128] = full * (1.0 / 96)

def correlate_kernel(y_ref, flags_ref, out_ref, keep_ref):
    @pl.when(pl.program_id(0) == 0)
    def _():
        keep_factor(flags_ref, keep_ref)
    keep = keep_ref[...]
    for i in range(CH):
        cols = y_ref[i]
        rows = cols[:, :128]
        turned = jnp.concatenate([rows[96:], -rows[:96]], axis=0)
        both = jnp.concatenate([rows, turned], axis=1)
        sums = lax.dot_general(both, cols, (((0,), (0,)), ((), ())), preferred_element_type=jnp.float32)
        out_ref[i, 0] = (sums[:128] * keep).astype(jnp.bfloat16)
        out_ref[i, 1] = (sums[128:] * keep).astype(jnp.bfloat16)

CH = 4
def correlate(spectra, flags):
    return pl.pallas_call(
        correlate_kernel, grid=(16 // CH,), out_shape=jax.ShapeDtypeStruct((16, 2, 128, 640), jnp.bfloat16),
        in_specs=[pl.BlockSpec((CH, 192, 640), lambda i: (i, 0, 0)), pl.BlockSpec((64, 512), lambda i: (0, 0))],
        out_specs=pl.BlockSpec((CH, 2, 128, 640), lambda i: (i, 0, 0, 0)),
        scratch_shapes=[pltpu.VMEM((128, 640), jnp.float32)],
        compiler_params=pltpu.CompilerParams(vmem_limit_bytes=58 * 2**20),
    )(spectra, flags)

def on_device(samples, chan_index, flags):
    spectra = exchange(chan_index, jnp.asarray(window_np()), samples)
    return correlate(spectra, flags)

def solution(mesh):
    return jax.shard_map(on_device, mesh=mesh, in_specs=(P(None, "stn", "chan"), P(), P("stn", None)),
                         out_specs=P("chan", None, "stn", None), check_vma=False)
```

time: 96.1 us -> 85.8 us (0.89); the launches traced: 94.4 us -> 85.6 us
  local copies, waits for them, and re-layouts: 5.24 us -> 0 us
  Pallas kernels: 88.9 us -> 85.6 us
    unnamed x6 -> x0, local copies, waits for them, and re-layouts: 3.63 us -> none
    pallas_call x2, Pallas kernels: 88.9 us -> 85.6 us  [the longest x1 78.6 us: exchange(): pl.pallas_call(exchange_kernel, out_shape=jax.ShapeDtypeStruct((16, 192,...]
where the time goes in v3:
time: 85.8 us; the launch traced here: 85.6 us
  Pallas kernels  85.6 us (100%)
    pallas_call x1, Pallas kernels, exchange(): pl.pallas_call(exchange_kernel, out_shape=jax.ShapeDtypeStruct((16, 192,...  78.6 us
    pallas_call x1, Pallas kernels, correlate(): pl.pallas_call(correlate_kernel, grid=(16 // CH,), out_shape=jax.ShapeDty...  6.97 us

profile of v3, /device:TPU:1, one launch (start us, length us, event | category | flops | bytes accessed | tf_op | source)
XLA Modules:
  0.0 85.6 jit_solution(5426018576771422735)
XLA Ops:
  0.0 78.6 %shard_map.46.y_ref = bf16[16,192,640]{2,1,0:T(8,128)(2,1)} custom-call(s32[1,512]{1,0:T(1,128)} %bitcast.1, f32[4,4096]{1,0:T(4,128)} %constant.2.clone.win_hbm, bf16[2,128,12288]{2,1,0:T(8,128)(2,1)} %x_hbm.1), custom_call_target="tpu_custom_call" | custom-call | tf_op jit(solution)/shard_map/pallas_call | solution.py:247
  78.6 7.0 %shard_map.47 = bf16[16,2,128,640]{3,2,1,0:T(8,128)(2,1)} custom-call(bf16[16,192,640]{2,1,0:T(8,128)(2,1)} %shard_map.46.y_ref, s32[64,512]{1,0:T(8,128)} %flags_ref.1), custom_call_target="tpu_custom_call" | custom-call | tf_op jit(solution)/shard_map/pallas_call | solution.py:286

commit v4 on v3

--- a/solution.py
+++ b/solution.py
@@ -119,9 +119,9 @@
     wcopy.wait()
     xcopy.wait()
 
-    def carry_copy(u, dest):
-        return pltpu.make_async_remote_copy(src_ref=cout_ref.at[u], dst_ref=cin_ref.at[u], send_sem=csend.at[u],
-                                            recv_sem=crecv.at[u], device_id=(dest, stn), device_id_type=MESH)
+    def carry_copy(u, h, dest):
+        return pltpu.make_async_remote_copy(src_ref=cout_ref.at[u, h], dst_ref=cin_ref.at[u, h], send_sem=csend.at[u, h],
+                                            recv_sem=crecv.at[u, h], device_id=(dest, stn), device_id_type=MESH)
 
     def keep_own(u):
         pltpu.make_async_copy(p_ref.at[u, chan], g_ref.at[0, u, chan], zrecv.at[u, zh * 4 + zl]).start()
@@ -152,15 +152,15 @@
 
     def carried_part(u):
         make_frames(u, True, win_ref, x_ref, f_ref)
-        for n0 in range(0, 512, NW):
-            re, im = half_dft(f_ref[...], tc_ref, ts_ref, n0, NW)
-            cout_ref[u, 0, :, n0:n0 + NW] = re.astype(jnp.bfloat16)
-            cout_ref[u, 1, :, n0:n0 + NW] = im.astype(jnp.bfloat16)
-        if u == UNITS[0]:
-            pl.semaphore_wait(barrier, 66)
-        @pl.when(chan < 31)
-        def _():
-            carry_copy(u, chan + 1).start()
+        for h in range(2):
+            re, im = half_dft(f_ref[...], tc_ref, ts_ref, h * NW, NW)
+            cout_ref[u, h, 0] = re.astype(jnp.bfloat16)
+            cout_ref[u, h, 1] = im.astype(jnp.bfloat16)
+            if u == UNITS[0] and h == 0:
+                pl.semaphore_wait(barrier, 66)
+            @pl.when(chan < 31)
+            def _():
+                carry_copy(u, h, chan + 1).start()
 
     def current_part(u):
         make_frames(u, False, win_ref, x_ref, f_ref)
@@ -170,17 +170,19 @@
             main_ref[1, :, n0:n0 + NW] = im
 
     def pieces(u):
-        @pl.when(chan == 0)
-        def _():
-            cin_ref[u] = jnp.zeros((2, 128, 512), jnp.bfloat16)
-        @pl.when(chan > 0)
-        def _():
-            carry_copy(u, chan).wait_recv()
-        for r in range(2):
-            full = main_ref[r] + cin_ref[u, r].astype(jnp.float32)
-            for cb in range(4):
-                blk = full[:, cb * 128:(cb + 1) * 128].T.astype(jnp.bfloat16)
-                p_ref[u, cb * 8:(cb + 1) * 8, r * 16:(r + 1) * 16, :] = blk.reshape(8, 16, 128)
+        for h in range(2):
+            @pl.when(chan == 0)
+            def _():
+                cin_ref[u, h] = jnp.zeros((2, 128, NW), jnp.bfloat16)
+            @pl.when(chan > 0)
+            def _():
+                carry_copy(u, h, chan).wait_recv()
+            for r in range(2):
+                full = main_ref[r, :, h * NW:(h + 1) * NW] + cin_ref[u, h, r].astype(jnp.float32)
+                for cb in range(2):
+                    blk = full[:, cb * 128:(cb + 1) * 128].T.astype(jnp.bfloat16)
+                    first_owner = h * 16 + cb * 8
+                    p_ref[u, first_owner:first_owner + 8, r * 16:(r + 1) * 16, :] = blk.reshape(8, 16, 128)
         keep_own(u)
 
     def own_blocks(u):
@@ -237,7 +239,8 @@
         pltpu.make_async_copy(v, v, zsend).wait()
         @pl.when(chan < 31)
         def _():
-            carry_copy(u, chan + 1).wait_send()
+            for h in range(2):
+                carry_copy(u, h, chan + 1).wait_send()
 
 NW = 256
 def exchange(ci, win, x):
@@ -249,9 +252,9 @@
         in_specs=[V, pl.BlockSpec(memory_space=pl.ANY), pl.BlockSpec(memory_space=pl.ANY)], out_specs=V,
         scratch_shapes=[pltpu.VMEM((5, 3, 32, 32, 128), bf), pltpu.VMEM((1024, 128), jnp.float32), pltpu.VMEM((TAPS, N), jnp.float32),
                         pltpu.VMEM((2, 128, 3 * N), bf), pltpu.VMEM((256, N), bf), pltpu.VMEM((N, 512), bf), pltpu.VMEM((N, 512), bf),
-                        pltpu.VMEM((2, 128, 512), jnp.float32), pltpu.VMEM((3, 2, 128, 512), bf), pltpu.VMEM((3, 2, 128, 512), bf),
+                        pltpu.VMEM((2, 128, 512), jnp.float32), pltpu.VMEM((3, 2, 2, 128, NW), bf), pltpu.VMEM((3, 2, 2, 128, NW), bf),
                         pltpu.VMEM((3, 32, 32, 128), bf),
-                        D, D, D((3,)), D((3,)), D, D((3, 8)), D, D((3,))],
+                        D, D, D((3, 2)), D((3, 2)), D, D((3, 8)), D, D((3,))],
         compiler_params=pltpu.CompilerParams(collective_id=0, has_side_effects=True, vmem_limit_bytes=58 * 2**20),
     )(ci.reshape(1, 512), win, x)
 

time: 85.8 us -> 92 us (1.072); the launches traced: 85.6 us -> 90.2 us
  Pallas kernels: 85.6 us -> 90.2 us
    pallas_call x1, Pallas kernels: 78.6 us -> 83.3 us  [exchange(): pl.pallas_call(exchange_kernel, out_shape=jax.ShapeDtypeStruct((16, 192,...]
where the time goes in v4:
time: 92 us; the launch traced here: 90.2 us
  Pallas kernels  90.2 us (98%)
    pallas_call x1, Pallas kernels, exchange(): pl.pallas_call(exchange_kernel, out_shape=jax.ShapeDtypeStruct((16, 192,...  83.3 us
    pallas_call x1, Pallas kernels, correlate(): pl.pallas_call(correlate_kernel, grid=(16 // CH,), out_shape=jax.ShapeDty...  6.97 us

profile of v4, /device:TPU:1, one launch (start us, length us, event | category | flops | bytes accessed | tf_op | source)
XLA Modules:
  0.0 90.2 jit_solution(3707133222260149870)
XLA Ops:
  0.0 83.3 %shard_map.46.y_ref = bf16[16,192,640]{2,1,0:T(8,128)(2,1)} custom-call(s32[1,512]{1,0:T(1,128)} %bitcast.1, f32[4,4096]{1,0:T(4,128)} %constant.2.clone.win_hbm, bf16[2,128,12288]{2,1,0:T(8,128)(2,1)} %x_hbm.1), custom_call_target="tpu_custom_call" | custom-call | tf_op jit(solution)/shard_map/pallas_call | solution.py:250
  83.3 7.0 %shard_map.47 = bf16[16,2,128,640]{3,2,1,0:T(8,128)(2,1)} custom-call(bf16[16,192,640]{2,1,0:T(8,128)(2,1)} %shard_map.46.y_ref, s32[64,512]{1,0:T(8,128)} %flags_ref.1), custom_call_target="tpu_custom_call" | custom-call | tf_op jit(solution)/shard_map/pallas_call | solution.py:289
